TPU v7x, 32 devices: a whole 2x2x4 slice. The times are simulated.
32 devices in a mesh: alpha: 8 (over y, x, core), beta: 4 (over z).
Axes of the slice: x: 2, y: 2, z: 4, core: 2. Of those that a mesh axis runs over, the one named last changes fastest.
Arguments:
- coeffs: bfloat16 [256, 512], P('alpha', 'beta'), may hold values from -6 to 6
- integrals: bfloat16 [400, 400], replicated, may hold values from -0.014953613 to 0.014953613
- source_beta: int32 [400, 512], P(None, 'beta'), may hold values from 0 to 511
- sign_beta: int32 [400, 512], P(None, 'beta'), may hold values from -1 to 1
- target_alpha: int32 [256, 400], P('alpha'), may hold values from 0 to 255
- sign_alpha: int32 [256, 400], P('alpha'), may hold values from -1 to 1
Outputs:
- sigma: float32 [256, 512], P('alpha', 'beta')
All inputs are finite; a program needn't handle non-finite values.
Results may differ from a plain program's by a relative error of at most 0.0029.
Values may be sent and summed in bfloat16 or wider, within the bound.
A program may use at most 64 MiB of HBM per device.

v0:
```python
import functools

import jax
import jax.numpy as jnp
from jax import lax
from jax.experimental import pallas as pl
from jax.experimental.pallas import tpu as pltpu
from jax.sharding import PartitionSpec as P

MESH = pl.DeviceIdType.MESH
LANES = 128
ROWS = 16


def kernel(
    n_alpha,
    n_beta,
    coeffs_ref,
    integrals_ref,
    source_ref,
    sign_b_ref,
    target_ref,
    sign_a_ref,
    out_ref,
    gathered,
    widened,
    excited,
    table,
    total,
    outgoing,
    incoming,
    gather_send,
    gather_recv,
    sum_send,
    sum_recv,
):
    rows, cols = coeffs_ref.shape
    pairs = integrals_ref.shape[0]
    all_alpha = rows * n_alpha
    ia = lax.axis_index("alpha")
    ib = lax.axis_index("beta")

    barrier = pltpu.get_barrier_semaphore()
    for d in range(1, n_beta):
        pl.semaphore_signal(
            barrier, inc=1, device_id=(ia, lax.rem(ib + d, n_beta)), device_id_type=MESH
        )
    for d in range(1, n_alpha):
        pl.semaphore_signal(
            barrier, inc=1, device_id=(lax.rem(ia + d, n_alpha), ib), device_id_type=MESH
        )
    pl.semaphore_wait(barrier, n_beta + n_alpha - 2)

    gather_copies = []
    for d in range(1, n_beta):
        copy = pltpu.make_async_remote_copy(
            src_ref=coeffs_ref,
            dst_ref=gathered.at[ib],
            send_sem=gather_send.at[d - 1],
            recv_sem=gather_recv.at[d - 1],
            device_id=(ia, lax.rem(ib + d, n_beta)),
            device_id_type=MESH,
        )
        copy.start()
        gather_copies.append(copy)
    gathered[ib] = coeffs_ref[...]

    def build(a, carry):
        targets = target_ref[pl.ds(a, 1), :]
        signs = sign_a_ref[pl.ds(a, 1), :].astype(jnp.float32)
        iota = lax.broadcasted_iota(jnp.int32, (all_alpha, pairs), 0)
        table[a] = jnp.where(targets == iota, signs, 0.0).astype(jnp.bfloat16)
        return carry

    lax.fori_loop(0, rows, build, 0)

    for copy in gather_copies:
        copy.wait()
    widened[...] = gathered[...].astype(jnp.float32)

    def excite(g, carry):
        start = pl.multiple_of(g * ROWS, ROWS)
        source = source_ref[pl.ds(start, ROWS), :]
        sign = sign_b_ref[pl.ds(start, ROWS), :].astype(jnp.float32)
        block = source // LANES
        lane = source - block * LANES
        masks = [block == j for j in range(n_beta * cols // LANES)]
        for a in range(rows):
            value = None
            for j in range(n_beta * cols // LANES):
                row = widened[j, a : a + 1, :]
                picked = jnp.take_along_axis(
                    jnp.broadcast_to(row, (ROWS, LANES)), lane, axis=1, mode="promise_in_bounds"
                )
                value = picked if j == 0 else jnp.where(masks[j], picked, value)
            excited[pl.ds(start, ROWS), a * cols : (a + 1) * cols] = (value * sign).astype(
                jnp.bfloat16
            )
        return carry

    lax.fori_loop(0, pairs // ROWS, excite, 0)

    total[...] = jnp.zeros_like(total)

    def contract(p, carry):
        start = pl.multiple_of(p * 2 * cols, 2 * cols)
        mixed = jnp.dot(
            integrals_ref[...],
            excited[:, pl.ds(start, 2 * cols)],
            preferred_element_type=jnp.float32,
        ).astype(jnp.bfloat16)
        total[...] += jnp.dot(
            table[2 * p], mixed[:, :cols], preferred_element_type=jnp.float32
        ) + jnp.dot(table[2 * p + 1], mixed[:, cols:], preferred_element_type=jnp.float32)
        return carry

    lax.fori_loop(0, rows // 2, contract, 0)

    for i in range(n_alpha):
        outgoing[i] = total[i * rows : (i + 1) * rows, :].astype(jnp.bfloat16)
    sum_copies = []
    for d in range(1, n_alpha):
        to = lax.rem(ia + d, n_alpha)
        copy = pltpu.make_async_remote_copy(
            src_ref=outgoing.at[to],
            dst_ref=incoming.at[d - 1],
            send_sem=sum_send.at[d - 1],
            recv_sem=sum_recv.at[d - 1],
            device_id=(to, ib),
            device_id_type=MESH,
        )
        copy.start()
        sum_copies.append(copy)
    result = total[pl.ds(pl.multiple_of(ia * rows, rows), rows), :]
    for d in range(1, n_alpha):
        sum_copies[d - 1].wait()
        result = result + incoming[d - 1].astype(jnp.float32)
    out_ref[...] = result


def on_device(coeffs, integrals, source_beta, sign_beta, target_alpha, sign_alpha):
    n_alpha = lax.axis_size("alpha")
    n_beta = lax.axis_size("beta")
    rows, cols = coeffs.shape
    pairs = integrals.shape[0]
    all_alpha = rows * n_alpha
    vmem = pl.BlockSpec(memory_space=pltpu.VMEM)
    return pl.pallas_call(
        functools.partial(kernel, n_alpha, n_beta),
        out_shape=jax.ShapeDtypeStruct((rows, cols), jnp.float32),
        in_specs=[vmem] * 6,
        out_specs=vmem,
        scratch_shapes=[
            pltpu.VMEM((n_beta, rows, cols), jnp.bfloat16),
            pltpu.VMEM((n_beta, rows, cols), jnp.float32),
            pltpu.VMEM((pairs, rows * cols), jnp.bfloat16),
            pltpu.VMEM((rows, all_alpha, pairs), jnp.bfloat16),
            pltpu.VMEM((all_alpha, cols), jnp.float32),
            pltpu.VMEM((n_alpha, rows, cols), jnp.bfloat16),
            pltpu.VMEM((n_alpha - 1, rows, cols), jnp.bfloat16),
            pltpu.SemaphoreType.DMA((n_beta - 1,)),
            pltpu.SemaphoreType.DMA((n_beta - 1,)),
            pltpu.SemaphoreType.DMA((n_alpha - 1,)),
            pltpu.SemaphoreType.DMA((n_alpha - 1,)),
        ],
        compiler_params=pltpu.CompilerParams(
            collective_id=0, has_side_effects=True, vmem_limit_bytes=48 * 1024 * 1024
        ),
    )(coeffs, integrals, source_beta, sign_beta, target_alpha, sign_alpha)


def solution(mesh):
    placed = (
        P("alpha", "beta"),
        P(),
        P(None, "beta"),
        P(None, "beta"),
        P("alpha", None),
        P("alpha", None),
    )
    return jax.shard_map(
        on_device, mesh=mesh, in_specs=placed, out_specs=P("alpha", "beta"), check_vma=False
    )
```

profile of v0, /device:TPU:0, one launch (start us, length us, event | category | flops | bytes accessed | tf_op | source)
XLA Modules:
  0.0 37.7 jit_solution(10058176386472628739)
XLA Ops:
  0.0 0.0 copy-start
  0.0 1.0 %copy-done = bf16[400,400]{1,0:T(8,128)(2,1)S(1)} copy-done((bf16[400,400]{1,0:T(8,128)(2,1)S(1)}, bf16[400,400]{1,0:T(8,128)(2,1)}, u32[]{:S(2)}) %copy-start) | copy-done | bytes 320024
  1.0 0.0 copy-start.1
  1.0 0.9 %copy-done.1 = s32[400,128]{1,0:T(8,128)S(1)} copy-done((s32[400,128]{1,0:T(8,128)S(1)}, s32[400,128]{1,0:T(8,128)}, u32[]{:S(2)}) %copy-start.1) | copy-done | bytes 204824
  1.9 0.0 copy-start.2
  1.9 0.9 %copy-done.2 = s32[400,128]{1,0:T(8,128)S(1)} copy-done((s32[400,128]{1,0:T(8,128)S(1)}, s32[400,128]{1,0:T(8,128)}, u32[]{:S(2)}) %copy-start.2) | copy-done | bytes 204824
  2.9 0.0 copy-start.3
  2.9 0.8 %copy-done.3 = s32[32,400]{1,0:T(8,128)S(1)} copy-done((s32[32,400]{1,0:T(8,128)S(1)}, s32[32,400]{1,0:T(8,128)}, u32[]{:S(2)}) %copy-start.3) | copy-done | bytes 51224
  3.7 0.0 copy-start.4
  3.7 0.8 %copy-done.4 = s32[32,400]{1,0:T(8,128)S(1)} copy-done((s32[32,400]{1,0:T(8,128)S(1)}, s32[32,400]{1,0:T(8,128)}, u32[]{:S(2)}) %copy-start.4) | copy-done | bytes 51224
  4.5 0.0 copy-start.5
  4.5 0.7 %copy-done.5 = bf16[32,128]{1,0:T(8,128)(2,1)S(1)} copy-done((bf16[32,128]{1,0:T(8,128)(2,1)S(1)}, bf16[32,128]{1,0:T(8,128)(2,1)}, u32[]{:S(2)}) %copy-start.5) | copy-done | bytes 8216
  5.2 31.9 %shard_map.64 = f32[32,128]{1,0:T(8,128)S(1)} custom-call(bf16[32,128]{1,0:T(8,128)(2,1)S(1)} %copy-done.5, bf16[400,400]{1,0:T(8,128)(2,1)S(1)} %copy-done, s32[400,128]{1,0:T(8,128)S(1)} %copy-done.1, s32[400,128]{1,0:T(8,128)S(1)} %copy-done.2, s32[32,400]{1,0:T(8,128)S(1)} %copy-done.3, s32[32,400]{1,0:T(8,128)S(1)} %copy-done.4), custom_call_target="tpu_custom_call" | custom-call | tf_op jit(solution)/shard_map/pallas_call | solution.py:148
  37.1 0.6 %copy.8 = f32[32,128]{1,0:T(8,128)} copy(f32[32,128]{1,0:T(8,128)S(1)} %shard_map.64) | data formatting | bytes 32768
Async XLA Ops:
  0.0 1.0 %copy-start = (bf16[400,400]{1,0:T(8,128)(2,1)S(1)}, bf16[400,400]{1,0:T(8,128)(2,1)}, u32[]{:S(2)}) copy-start(bf16[400,400]{1,0:T(8,128)(2,1)} %integrals_ref.1) | copy-start | bytes 960004
  1.0 0.9 %copy-start.1 = (s32[400,128]{1,0:T(8,128)S(1)}, s32[400,128]{1,0:T(8,128)}, u32[]{:S(2)}) copy-start(s32[400,128]{1,0:T(8,128)} %source_ref.1) | copy-start | bytes 614404
  1.9 0.9 %copy-start.2 = (s32[400,128]{1,0:T(8,128)S(1)}, s32[400,128]{1,0:T(8,128)}, u32[]{:S(2)}) copy-start(s32[400,128]{1,0:T(8,128)} %sign_b_ref.1) | copy-start | bytes 614404
  2.9 0.8 %copy-start.3 = (s32[32,400]{1,0:T(8,128)S(1)}, s32[32,400]{1,0:T(8,128)}, u32[]{:S(2)}) copy-start(s32[32,400]{1,0:T(8,128)} %target_ref.1) | copy-start | bytes 153604
  3.7 0.8 %copy-start.4 = (s32[32,400]{1,0:T(8,128)S(1)}, s32[32,400]{1,0:T(8,128)}, u32[]{:S(2)}) copy-start(s32[32,400]{1,0:T(8,128)} %sign_a_ref.1) | copy-start | bytes 153604
  4.5 0.7 %copy-start.5 = (bf16[32,128]{1,0:T(8,128)(2,1)S(1)}, bf16[32,128]{1,0:T(8,128)(2,1)}, u32[]{:S(2)}) copy-start(bf16[32,128]{1,0:T(8,128)(2,1)} %coeffs_ref.1) | copy-start | bytes 24580
where the time goes:
time: 38.1 us; the launch traced here: 37.7 us
  Pallas kernels  31.9 us (84%)
  local copies, waits for them, and re-layouts  5.84 us (15%)
    pallas_call x1, Pallas kernels, on_device(): pl.pallas_call(functools.partial(kernel, n_alpha, n_beta), out_shape=jax....  31.9 us
    unnamed x13, local copies, waits for them, and re-layouts  5.84 us

commit v1 on v0

v1 whole, which is shorter than its diff:
```python
import functools

import jax
import jax.numpy as jnp
from jax import lax
from jax.experimental import pallas as pl
from jax.experimental.pallas import tpu as pltpu
from jax.sharding import PartitionSpec as P

MESH = pl.DeviceIdType.MESH
LANES = 128
ROWS = 16


def spread_gather(values, lanes):
    numbers = lax.GatherDimensionNumbers(
        offset_dims=(),
        collapsed_slice_dims=(1,),
        start_index_map=(1,),
        operand_batching_dims=(0,),
        start_indices_batching_dims=(0,),
    )
    return lax.gather(
        values,
        lanes[:, :, None],
        numbers,
        slice_sizes=(1, 1),
        mode=lax.GatherScatterMode.PROMISE_IN_BOUNDS,
    )


def kernel(
    n_alpha,
    n_beta,
    coeffs_hbm,
    integrals_hbm,
    source_hbm,
    sign_b_hbm,
    target_hbm,
    sign_a_hbm,
    out_ref,
    integrals_ref,
    source_ref,
    sign_b_ref,
    target_ref,
    sign_a_ref,
    gathered,
    spread,
    lane_ref,
    block_ref,
    sign_ref,
    excited_0,
    excited_1,
    mixed_0,
    mixed_1,
    table,
    total,
    outgoing,
    incoming,
    load_sem,
    gather_send,
    gather_recv,
    sum_send,
    sum_recv,
):
    rows, cols = coeffs_hbm.shape
    pairs = integrals_hbm.shape[0]
    all_alpha = rows * n_alpha
    blocks = n_beta * cols // LANES
    ia = lax.axis_index("alpha")
    ib = lax.axis_index("beta")

    barrier = pltpu.get_barrier_semaphore()
    for d in range(1, n_beta):
        pl.semaphore_signal(
            barrier, inc=1, device_id=(ia, lax.rem(ib + d, n_beta)), device_id_type=MESH
        )
    for d in range(1, n_alpha):
        pl.semaphore_signal(
            barrier, inc=1, device_id=(lax.rem(ia + d, n_alpha), ib), device_id_type=MESH
        )
    loads = [
        pltpu.make_async_copy(src, dst, load_sem.at[i])
        for i, (src, dst) in enumerate(
            (
                (target_hbm, target_ref),
                (sign_a_hbm, sign_a_ref),
                (source_hbm, source_ref),
                (sign_b_hbm, sign_b_ref),
                (coeffs_hbm, gathered.at[ib]),
                (integrals_hbm, integrals_ref),
            )
        )
    ]
    for load in loads:
        load.start()
    pl.semaphore_wait(barrier, n_beta + n_alpha - 2)

    gather_copies = []
    for d in range(1, n_beta):
        copy = pltpu.make_async_remote_copy(
            src_ref=coeffs_hbm,
            dst_ref=gathered.at[ib],
            send_sem=gather_send.at[d - 1],
            recv_sem=gather_recv.at[d - 1],
            device_id=(ia, lax.rem(ib + d, n_beta)),
            device_id_type=MESH,
        )
        copy.start()
        gather_copies.append(copy)

    loads[0].wait()
    loads[1].wait()
    iota = lax.broadcasted_iota(jnp.int32, (ROWS, pairs), 0)

    def build(a, carry):
        targets = (jnp.broadcast_to(target_ref[pl.ds(a, 1), :], (ROWS, pairs)) - iota).astype(
            jnp.int16
        )
        signs = (
            jnp.broadcast_to(sign_a_ref[pl.ds(a, 1), :], (ROWS, pairs))
            .astype(jnp.float32)
            .astype(jnp.bfloat16)
        )
        zero = jnp.zeros_like(signs)
        for i in range(all_alpha // ROWS):
            table[a, i * ROWS : (i + 1) * ROWS, :] = jnp.where(
                targets == jnp.int16(i * ROWS), signs, zero
            )
        return carry

    lax.fori_loop(0, rows, build, 0)

    loads[2].wait()
    loads[3].wait()
    source = source_ref[...]
    block = source // LANES
    lane_ref[...] = (source - block * LANES).astype(jnp.int16)
    block_ref[...] = block.astype(jnp.int16)
    sign_ref[...] = sign_b_ref[...].astype(jnp.float32).astype(jnp.bfloat16)
    total[...] = jnp.zeros_like(total)

    loads[4].wait()
    loads[5].wait()
    for copy in gather_copies:
        copy.wait()

    for j in range(blocks):
        for a in range(rows):
            spread[j, a] = jnp.broadcast_to(
                gathered[j, a : a + 1, :].astype(jnp.float32), (ROWS, LANES)
            ).astype(jnp.bfloat16)

    def excite(p, out):
        for g in range(pairs // ROWS):
            at = slice(g * ROWS, (g + 1) * ROWS)
            lane = lane_ref[at, :]
            block = block_ref[at, :]
            sign = sign_ref[at, :]
            masks = [block == jnp.int16(j) for j in range(blocks)]
            for i in range(2):
                value = None
                for j in range(blocks):
                    picked = spread_gather(spread[j, 2 * p + i], lane)
                    value = picked if j == 0 else jnp.where(masks[j], picked, value)
                out[at, i * cols : (i + 1) * cols] = value * sign

    def contract(src, out):
        out[...] = jnp.dot(
            integrals_ref[...], src[...], preferred_element_type=jnp.float32
        ).astype(jnp.bfloat16)

    def scatter(p, src):
        total[...] += jnp.dot(
            table[2 * p], src[:, :cols], preferred_element_type=jnp.float32
        ) + jnp.dot(table[2 * p + 1], src[:, cols:], preferred_element_type=jnp.float32)

    excite(0, excited_0)
    contract(excited_0, mixed_0)
    excite(1, excited_1)

    def step(s, carry):
        p = 2 * s
        excite(p + 2, excited_0)
        contract(excited_1, mixed_1)
        scatter(p, mixed_0)
        excite(p + 3, excited_1)
        contract(excited_0, mixed_0)
        scatter(p + 1, mixed_1)
        return carry

    lax.fori_loop(0, rows // 4 - 1, step, 0)
    contract(excited_1, mixed_1)
    scatter(rows // 2 - 2, mixed_0)
    scatter(rows // 2 - 1, mixed_1)

    for i in range(n_alpha):
        outgoing[i] = total[i * rows : (i + 1) * rows, :].astype(jnp.bfloat16)
    sum_copies = []
    for d in range(1, n_alpha):
        to = lax.rem(ia + d, n_alpha)
        copy = pltpu.make_async_remote_copy(
            src_ref=outgoing.at[to],
            dst_ref=incoming.at[d - 1],
            send_sem=sum_send.at[d - 1],
            recv_sem=sum_recv.at[d - 1],
            device_id=(to, ib),
            device_id_type=MESH,
        )
        copy.start()
        sum_copies.append(copy)
    result = total[pl.ds(pl.multiple_of(ia * rows, rows), rows), :]
    for d in range(1, n_alpha):
        sum_copies[d - 1].wait()
        result = result + incoming[d - 1].astype(jnp.float32)
    out_ref[...] = result


def on_device(coeffs, integrals, source_beta, sign_beta, target_alpha, sign_alpha):
    n_alpha = lax.axis_size("alpha")
    n_beta = lax.axis_size("beta")
    rows, cols = coeffs.shape
    pairs = integrals.shape[0]
    all_alpha = rows * n_alpha
    blocks = n_beta * cols // LANES
    return pl.pallas_call(
        functools.partial(kernel, n_alpha, n_beta),
        out_shape=jax.ShapeDtypeStruct((rows, cols), jnp.float32),
        in_specs=[pl.BlockSpec(memory_space=pl.ANY)] * 6,
        out_specs=pl.BlockSpec(memory_space=pltpu.VMEM),
        scratch_shapes=[
            pltpu.VMEM((pairs, pairs), jnp.bfloat16),
            pltpu.VMEM((pairs, cols), jnp.int32),
            pltpu.VMEM((pairs, cols), jnp.int32),
            pltpu.VMEM((rows, pairs), jnp.int32),
            pltpu.VMEM((rows, pairs), jnp.int32),
            pltpu.VMEM((n_beta, rows, cols), jnp.bfloat16),
            pltpu.VMEM((blocks, rows, ROWS, LANES), jnp.bfloat16),
            pltpu.VMEM((pairs, cols), jnp.int16),
            pltpu.VMEM((pairs, cols), jnp.int16),
            pltpu.VMEM((pairs, cols), jnp.bfloat16),
            pltpu.VMEM((pairs, 2 * cols), jnp.bfloat16),
            pltpu.VMEM((pairs, 2 * cols), jnp.bfloat16),
            pltpu.VMEM((pairs, 2 * cols), jnp.bfloat16),
            pltpu.VMEM((pairs, 2 * cols), jnp.bfloat16),
            pltpu.VMEM((rows, all_alpha, pairs), jnp.bfloat16),
            pltpu.VMEM((all_alpha, cols), jnp.float32),
            pltpu.VMEM((n_alpha, rows, cols), jnp.bfloat16),
            pltpu.VMEM((n_alpha - 1, rows, cols), jnp.bfloat16),
            pltpu.SemaphoreType.DMA((6,)),
            pltpu.SemaphoreType.DMA((n_beta - 1,)),
            pltpu.SemaphoreType.DMA((n_beta - 1,)),
            pltpu.SemaphoreType.DMA((n_alpha - 1,)),
            pltpu.SemaphoreType.DMA((n_alpha - 1,)),
        ],
        compiler_params=pltpu.CompilerParams(
            collective_id=0, has_side_effects=True, vmem_limit_bytes=56 * 1024 * 1024
        ),
    )(coeffs, integrals, source_beta, sign_beta, target_alpha, sign_alpha)


def solution(mesh):
    placed = (
        P("alpha", "beta"),
        P(),
        P(None, "beta"),
        P(None, "beta"),
        P("alpha", None),
        P("alpha", None),
    )
    return jax.shard_map(
        on_device, mesh=mesh, in_specs=placed, out_specs=P("alpha", "beta"), check_vma=False
    )
```

time: 38.1 us -> 21 us (0.55)
  Pallas kernels: 31.9 us -> 19.5 us
  local copies, waits for them, and re-layouts: 5.84 us -> 1.32 us
    pallas_call x1, Pallas kernels: 31.9 us -> 19.5 us  [on_device(): pl.pallas_call(functools.partial(kernel, n_alpha, n_beta), out_shape=jax....]
    unnamed x13 -> x1, local copies, waits for them, and re-layouts: 5.84 us -> 1.32 us
where the time goes in v1:
time: 21 us; the launch traced here: 20.8 us
  Pallas kernels  19.5 us (93%)
  local copies, waits for them, and re-layouts  1.32 us (6%)
    pallas_call x1, Pallas kernels, on_device(): pl.pallas_call(functools.partial(kernel, n_alpha, n_beta), out_shape=jax....  19.5 us
    unnamed x1, local copies, waits for them, and re-layouts  1.32 us

profile of v1, /device:TPU:0, one launch (start us, length us, event | category | flops | bytes accessed | tf_op | source)
XLA Modules:
  0.0 20.8 jit_solution(4204738571730998837)
XLA Ops:
  0.0 19.5 %shard_map.64 = f32[32,128]{1,0:T(8,128)} custom-call(bf16[32,128]{1,0:T(8,128)(2,1)} %coeffs_hbm.1, bf16[400,400]{1,0:T(8,128)(2,1)} %integrals_hbm.1, s32[400,128]{1,0:T(8,128)} %source_hbm.1, s32[400,128]{1,0:T(8,128)} %sign_b_hbm.1, s32[32,400]{1,0:T(8,128)} %target_hbm.1, s32[32,400]{1,0:T(8,128)} %sign_a_hbm.1), custom_call_target="tpu_custom_call" | custom-call | tf_op jit(solution)/shard_map/pallas_call | solution.py:226
  19.5 1.3 %copy.8 = f32[32,128]{1,0:T(8,128)} copy(f32[32,128]{1,0:T(8,128)} %shard_map.64) | data formatting | bytes 32768

commit v2 on v1

--- a/solution.py
+++ b/solution.py
@@ -47,13 +47,15 @@
     gathered,
     spread,
     lane_ref,
-    block_ref,
+    slot_ref,
     sign_ref,
+    base,
     excited_0,
     excited_1,
     mixed_0,
     mixed_1,
-    table,
+    table_0,
+    table_1,
     total,
     outgoing,
     incoming,
@@ -66,7 +68,6 @@
     rows, cols = coeffs_hbm.shape
     pairs = integrals_hbm.shape[0]
     all_alpha = rows * n_alpha
-    blocks = n_beta * cols // LANES
     ia = lax.axis_index("alpha")
     ib = lax.axis_index("beta")
 
@@ -83,11 +84,11 @@
         pltpu.make_async_copy(src, dst, load_sem.at[i])
         for i, (src, dst) in enumerate(
             (
+                (coeffs_hbm, gathered.at[0]),
+                (source_hbm, source_ref),
+                (sign_b_hbm, sign_b_ref),
                 (target_hbm, target_ref),
                 (sign_a_hbm, sign_a_ref),
-                (source_hbm, source_ref),
-                (sign_b_hbm, sign_b_ref),
-                (coeffs_hbm, gathered.at[ib]),
                 (integrals_hbm, integrals_ref),
             )
         )
@@ -100,7 +101,7 @@
     for d in range(1, n_beta):
         copy = pltpu.make_async_remote_copy(
             src_ref=coeffs_hbm,
-            dst_ref=gathered.at[ib],
+            dst_ref=gathered.at[d],
             send_sem=gather_send.at[d - 1],
             recv_sem=gather_recv.at[d - 1],
             device_id=(ia, lax.rem(ib + d, n_beta)),
@@ -111,58 +112,52 @@
 
     loads[0].wait()
     loads[1].wait()
-    iota = lax.broadcasted_iota(jnp.int32, (ROWS, pairs), 0)
-
-    def build(a, carry):
-        targets = (jnp.broadcast_to(target_ref[pl.ds(a, 1), :], (ROWS, pairs)) - iota).astype(
-            jnp.int16
-        )
-        signs = (
-            jnp.broadcast_to(sign_a_ref[pl.ds(a, 1), :], (ROWS, pairs))
-            .astype(jnp.float32)
-            .astype(jnp.bfloat16)
-        )
-        zero = jnp.zeros_like(signs)
-        for i in range(all_alpha // ROWS):
-            table[a, i * ROWS : (i + 1) * ROWS, :] = jnp.where(
-                targets == jnp.int16(i * ROWS), signs, zero
-            )
-        return carry
-
-    lax.fori_loop(0, rows, build, 0)
-
-    loads[2].wait()
-    loads[3].wait()
     source = source_ref[...]
     block = source // LANES
     lane_ref[...] = (source - block * LANES).astype(jnp.int16)
-    block_ref[...] = block.astype(jnp.int16)
+    slot = ib - block
+    slot_ref[...] = jnp.where(slot < 0, slot + n_beta, slot).astype(jnp.int16)
+
+    def spread_rows(d):
+        for a in range(rows):
+            spread[d, a] = jnp.broadcast_to(
+                gathered[d, a : a + 1, :].astype(jnp.float32), (ROWS, LANES)
+            ).astype(jnp.bfloat16)
+
+    spread_rows(0)
+
+    def excite_own(g, carry):
+        at = pl.ds(pl.multiple_of(g * ROWS, ROWS), ROWS)
+        lane = lane_ref[at, :]
+        for a in range(rows):
+            base[a // 2, at, (a % 2) * cols : (a % 2 + 1) * cols] = spread_gather(
+                spread[0, a], lane
+            )
+        return carry
+
+    lax.fori_loop(0, pairs // ROWS, excite_own, 0)
+
+    loads[2].wait()
     sign_ref[...] = sign_b_ref[...].astype(jnp.float32).astype(jnp.bfloat16)
     total[...] = jnp.zeros_like(total)
-
-    loads[4].wait()
-    loads[5].wait()
+    for load in loads[3:]:
+        load.wait()
     for copy in gather_copies:
         copy.wait()
-
-    for j in range(blocks):
-        for a in range(rows):
-            spread[j, a] = jnp.broadcast_to(
-                gathered[j, a : a + 1, :].astype(jnp.float32), (ROWS, LANES)
-            ).astype(jnp.bfloat16)
+    for d in range(1, n_beta):
+        spread_rows(d)
 
     def excite(p, out):
         for g in range(pairs // ROWS):
             at = slice(g * ROWS, (g + 1) * ROWS)
             lane = lane_ref[at, :]
-            block = block_ref[at, :]
+            slot = slot_ref[at, :]
             sign = sign_ref[at, :]
-            masks = [block == jnp.int16(j) for j in range(blocks)]
+            masks = [slot == jnp.int16(d) for d in range(n_beta)]
             for i in range(2):
-                value = None
-                for j in range(blocks):
-                    picked = spread_gather(spread[j, 2 * p + i], lane)
-                    value = picked if j == 0 else jnp.where(masks[j], picked, value)
+                value = base[p, at, i * cols : (i + 1) * cols]
+                for d in range(1, n_beta):
+                    value = jnp.where(masks[d], spread_gather(spread[d, 2 * p + i], lane), value)
                 out[at, i * cols : (i + 1) * cols] = value * sign
 
     def contract(src, out):
@@ -170,29 +165,50 @@
             integrals_ref[...], src[...], preferred_element_type=jnp.float32
         ).astype(jnp.bfloat16)
 
-    def scatter(p, src):
+    iota = lax.broadcasted_iota(jnp.int32, (ROWS, pairs), 0)
+
+    def build(p, out):
+        for i in range(2):
+            row = pl.ds(2 * p + i, 1)
+            targets = (jnp.broadcast_to(target_ref[row, :], (ROWS, pairs)) - iota).astype(jnp.int16)
+            signs = (
+                jnp.broadcast_to(sign_a_ref[row, :], (ROWS, pairs))
+                .astype(jnp.float32)
+                .astype(jnp.bfloat16)
+            )
+            zero = jnp.zeros_like(signs)
+            for k in range(all_alpha // ROWS):
+                out[i, k * ROWS : (k + 1) * ROWS, :] = jnp.where(
+                    targets == jnp.int16(k * ROWS), signs, zero
+                )
+
+    def scatter(table, src):
         total[...] += jnp.dot(
-            table[2 * p], src[:, :cols], preferred_element_type=jnp.float32
-        ) + jnp.dot(table[2 * p + 1], src[:, cols:], preferred_element_type=jnp.float32)
+            table[0], src[:, :cols], preferred_element_type=jnp.float32
+        ) + jnp.dot(table[1], src[:, cols:], preferred_element_type=jnp.float32)
 
     excite(0, excited_0)
     contract(excited_0, mixed_0)
+    build(0, table_0)
     excite(1, excited_1)
 
     def step(s, carry):
         p = 2 * s
         excite(p + 2, excited_0)
         contract(excited_1, mixed_1)
-        scatter(p, mixed_0)
+        build(p + 1, table_1)
+        scatter(table_0, mixed_0)
         excite(p + 3, excited_1)
         contract(excited_0, mixed_0)
-        scatter(p + 1, mixed_1)
+        build(p + 2, table_0)
+        scatter(table_1, mixed_1)
         return carry
 
     lax.fori_loop(0, rows // 4 - 1, step, 0)
     contract(excited_1, mixed_1)
-    scatter(rows // 2 - 2, mixed_0)
-    scatter(rows // 2 - 1, mixed_1)
+    build(rows // 2 - 1, table_1)
+    scatter(table_0, mixed_0)
+    scatter(table_1, mixed_1)
 
     for i in range(n_alpha):
         outgoing[i] = total[i * rows : (i + 1) * rows, :].astype(jnp.bfloat16)
@@ -222,11 +238,14 @@
     rows, cols = coeffs.shape
     pairs = integrals.shape[0]
     all_alpha = rows * n_alpha
-    blocks = n_beta * cols // LANES
+    operands = [
+        pltpu.with_memory_space_constraint(array, pltpu.HBM)
+        for array in (coeffs, integrals, source_beta, sign_beta, target_alpha, sign_alpha)
+    ]
     return pl.pallas_call(
         functools.partial(kernel, n_alpha, n_beta),
         out_shape=jax.ShapeDtypeStruct((rows, cols), jnp.float32),
-        in_specs=[pl.BlockSpec(memory_space=pl.ANY)] * 6,
+        in_specs=[pl.BlockSpec(memory_space=pltpu.HBM)] * 6,
         out_specs=pl.BlockSpec(memory_space=pltpu.VMEM),
         scratch_shapes=[
             pltpu.VMEM((pairs, pairs), jnp.bfloat16),
@@ -235,15 +254,17 @@
             pltpu.VMEM((rows, pairs), jnp.int32),
             pltpu.VMEM((rows, pairs), jnp.int32),
             pltpu.VMEM((n_beta, rows, cols), jnp.bfloat16),
-            pltpu.VMEM((blocks, rows, ROWS, LANES), jnp.bfloat16),
+            pltpu.VMEM((n_beta, rows, ROWS, LANES), jnp.bfloat16),
             pltpu.VMEM((pairs, cols), jnp.int16),
             pltpu.VMEM((pairs, cols), jnp.int16),
             pltpu.VMEM((pairs, cols), jnp.bfloat16),
-            pltpu.VMEM((pairs, 2 * cols), jnp.bfloat16),
-            pltpu.VMEM((pairs, 2 * cols), jnp.bfloat16),
-            pltpu.VMEM((pairs, 2 * cols), jnp.bfloat16),
-            pltpu.VMEM((pairs, 2 * cols), jnp.bfloat16),
-            pltpu.VMEM((rows, all_alpha, pairs), jnp.bfloat16),
+            pltpu.VMEM((rows // 2, pairs, 2 * cols), jnp.bfloat16),
+            pltpu.VMEM((pairs, 2 * cols), jnp.bfloat16),
+            pltpu.VMEM((pairs, 2 * cols), jnp.bfloat16),
+            pltpu.VMEM((pairs, 2 * cols), jnp.bfloat16),
+            pltpu.VMEM((pairs, 2 * cols), jnp.bfloat16),
+            pltpu.VMEM((2, all_alpha, pairs), jnp.bfloat16),
+            pltpu.VMEM((2, all_alpha, pairs), jnp.bfloat16),
             pltpu.VMEM((all_alpha, cols), jnp.float32),
             pltpu.VMEM((n_alpha, rows, cols), jnp.bfloat16),
             pltpu.VMEM((n_alpha - 1, rows, cols), jnp.bfloat16),
@@ -254,9 +275,9 @@
             pltpu.SemaphoreType.DMA((n_alpha - 1,)),
         ],
         compiler_params=pltpu.CompilerParams(
-            collective_id=0, has_side_effects=True, vmem_limit_bytes=56 * 1024 * 1024
+            collective_id=0, has_side_effects=True, vmem_limit_bytes=32 * 1024 * 1024
         ),
-    )(coeffs, integrals, source_beta, sign_beta, target_alpha, sign_alpha)
+    )(*operands)
 
 
 def solution(mesh):

time: 21 us -> 19.8 us (0.943)
  local copies, waits for them, and re-layouts: 1.32 us -> 0.61 us
  Pallas kernels: 19.5 us -> 19 us
    unnamed x1, local copies, waits for them, and re-layouts: 1.32 us -> 0.61 us
    pallas_call x1, Pallas kernels: 19.5 us -> 19 us  [on_device(): pl.pallas_call(functools.partial(kernel, n_alpha, n_beta), out_shape=jax....]
where the time goes in v2:
time: 19.8 us; the launch traced here: 19.6 us
  Pallas kernels  19 us (96%)
  local copies, waits for them, and re-layouts  0.61 us (3%)
    pallas_call x1, Pallas kernels, on_device(): pl.pallas_call(functools.partial(kernel, n_alpha, n_beta), out_shape=jax....  19 us
    unnamed x1, local copies, waits for them, and re-layouts  0.61 us

profile of v2, /device:TPU:0, one launch (start us, length us, event | category | flops | bytes accessed | tf_op | source)
XLA Modules:
  0.0 19.6 jit_solution(9395986045161483038)
XLA Ops:
  0.0 19.0 %shard_map.64 = f32[32,128]{1,0:T(8,128)S(1)} custom-call(bf16[32,128]{1,0:T(8,128)(2,1)} %coeffs_hbm.1, bf16[400,400]{1,0:T(8,128)(2,1)} %integrals_hbm.1, s32[400,128]{1,0:T(8,128)} %source_hbm.1, s32[400,128]{1,0:T(8,128)} %sign_b_hbm.1, s32[32,400]{1,0:T(8,128)} %target_hbm.1, s32[32,400]{1,0:T(8,128)} %sign_a_hbm.1), custom_call_target="tpu_custom_call" | custom-call | tf_op jit(solution)/shard_map/pallas_call | solution.py:245
  19.0 0.6 %copy.8 = f32[32,128]{1,0:T(8,128)} copy(f32[32,128]{1,0:T(8,128)S(1)} %shard_map.64) | data formatting | bytes 32768

commit v3 on v2

--- a/solution.py
+++ b/solution.py
@@ -147,8 +147,10 @@
     for d in range(1, n_beta):
         spread_rows(d)
 
-    def excite(p, out):
-        for g in range(pairs // ROWS):
+    groups = pairs // ROWS
+
+    def excite(p, out, first=0, last=groups):
+        for g in range(first, last):
             at = slice(g * ROWS, (g + 1) * ROWS)
             lane = lane_ref[at, :]
             slot = slot_ref[at, :]
@@ -167,48 +169,56 @@
 
     iota = lax.broadcasted_iota(jnp.int32, (ROWS, pairs), 0)
 
-    def build(p, out):
-        for i in range(2):
-            row = pl.ds(2 * p + i, 1)
-            targets = (jnp.broadcast_to(target_ref[row, :], (ROWS, pairs)) - iota).astype(jnp.int16)
-            signs = (
-                jnp.broadcast_to(sign_a_ref[row, :], (ROWS, pairs))
-                .astype(jnp.float32)
-                .astype(jnp.bfloat16)
+    def build(p, out, i):
+        row = pl.ds(2 * p + i, 1)
+        targets = (jnp.broadcast_to(target_ref[row, :], (ROWS, pairs)) - iota).astype(jnp.int16)
+        signs = (
+            jnp.broadcast_to(sign_a_ref[row, :], (ROWS, pairs))
+            .astype(jnp.float32)
+            .astype(jnp.bfloat16)
+        )
+        zero = jnp.zeros_like(signs)
+        for k in range(all_alpha // ROWS):
+            out[i, k * ROWS : (k + 1) * ROWS, :] = jnp.where(
+                targets == jnp.int16(k * ROWS), signs, zero
             )
-            zero = jnp.zeros_like(signs)
-            for k in range(all_alpha // ROWS):
-                out[i, k * ROWS : (k + 1) * ROWS, :] = jnp.where(
-                    targets == jnp.int16(k * ROWS), signs, zero
-                )
-
-    def scatter(table, src):
+
+    def scatter(table, src, i):
         total[...] += jnp.dot(
-            table[0], src[:, :cols], preferred_element_type=jnp.float32
-        ) + jnp.dot(table[1], src[:, cols:], preferred_element_type=jnp.float32)
+            table[i], src[:, i * cols : (i + 1) * cols], preferred_element_type=jnp.float32
+        )
+
+    third = -(-groups // 3)
+
+    def stages(p, here, there, mixed, mixed_next, table, table_next):
+        contract(there, mixed_next)
+        excite(p + 2, here, 0, third)
+        build(p + 1, table_next, 0)
+        scatter(table, mixed, 0)
+        excite(p + 2, here, third, 2 * third)
+        build(p + 1, table_next, 1)
+        scatter(table, mixed, 1)
+        excite(p + 2, here, 2 * third, groups)
 
     excite(0, excited_0)
     contract(excited_0, mixed_0)
-    build(0, table_0)
+    build(0, table_0, 0)
+    build(0, table_0, 1)
     excite(1, excited_1)
 
     def step(s, carry):
         p = 2 * s
-        excite(p + 2, excited_0)
-        contract(excited_1, mixed_1)
-        build(p + 1, table_1)
-        scatter(table_0, mixed_0)
-        excite(p + 3, excited_1)
-        contract(excited_0, mixed_0)
-        build(p + 2, table_0)
-        scatter(table_1, mixed_1)
+        stages(p, excited_0, excited_1, mixed_0, mixed_1, table_0, table_1)
+        stages(p + 1, excited_1, excited_0, mixed_1, mixed_0, table_1, table_0)
         return carry
 
     lax.fori_loop(0, rows // 4 - 1, step, 0)
     contract(excited_1, mixed_1)
-    build(rows // 2 - 1, table_1)
-    scatter(table_0, mixed_0)
-    scatter(table_1, mixed_1)
+    build(rows // 2 - 1, table_1, 0)
+    build(rows // 2 - 1, table_1, 1)
+    for table, mixed in ((table_0, mixed_0), (table_1, mixed_1)):
+        scatter(table, mixed, 0)
+        scatter(table, mixed, 1)
 
     for i in range(n_alpha):
         outgoing[i] = total[i * rows : (i + 1) * rows, :].astype(jnp.bfloat16)

time: 19.8 us -> 19.7 us (level)
  no operation moved by 1% of the time
where the time goes in v3:
time: 19.7 us; the launch traced here: 19.6 us
  Pallas kernels  19 us (96%)
  local copies, waits for them, and re-layouts  0.61 us (3%)
    pallas_call x1, Pallas kernels, on_device(): pl.pallas_call(functools.partial(kernel, n_alpha, n_beta), out_shape=jax....  19 us
    unnamed x1, local copies, waits for them, and re-layouts  0.61 us

profile of v3, /device:TPU:0, one launch (start us, length us, event | category | flops | bytes accessed | tf_op | source)
XLA Modules:
  0.0 19.6 jit_solution(10975643455367366470)
XLA Ops:
  0.0 19.0 %shard_map.64 = f32[32,128]{1,0:T(8,128)S(1)} custom-call(bf16[32,128]{1,0:T(8,128)(2,1)} %coeffs_hbm.1, bf16[400,400]{1,0:T(8,128)(2,1)} %integrals_hbm.1, s32[400,128]{1,0:T(8,128)} %source_hbm.1, s32[400,128]{1,0:T(8,128)} %sign_b_hbm.1, s32[32,400]{1,0:T(8,128)} %target_hbm.1, s32[32,400]{1,0:T(8,128)} %sign_a_hbm.1), custom_call_target="tpu_custom_call" | custom-call | tf_op jit(solution)/shard_map/pallas_call | solution.py:255
  19.0 0.6 %copy.8 = f32[32,128]{1,0:T(8,128)} copy(f32[32,128]{1,0:T(8,128)S(1)} %shard_map.64) | data formatting | bytes 32768

commit v4 on v3

--- a/solution.py
+++ b/solution.py
@@ -10,6 +10,7 @@
 MESH = pl.DeviceIdType.MESH
 LANES = 128
 ROWS = 16
+WIDE = 4
 
 
 def spread_gather(values, lanes):
@@ -44,6 +45,8 @@
     sign_b_ref,
     target_ref,
     sign_a_ref,
+    target_flat,
+    sign_a_flat,
     gathered,
     spread,
     lane_ref,
@@ -71,6 +74,8 @@
     ia = lax.axis_index("alpha")
     ib = lax.axis_index("beta")
 
+    sets = rows // WIDE
+
     barrier = pltpu.get_barrier_semaphore()
     for d in range(1, n_beta):
         pl.semaphore_signal(
@@ -130,7 +135,7 @@
         at = pl.ds(pl.multiple_of(g * ROWS, ROWS), ROWS)
         lane = lane_ref[at, :]
         for a in range(rows):
-            base[a // 2, at, (a % 2) * cols : (a % 2 + 1) * cols] = spread_gather(
+            base[a % sets, at, (a // sets) * cols : (a // sets + 1) * cols] = spread_gather(
                 spread[0, a], lane
             )
         return carry
@@ -142,6 +147,10 @@
     total[...] = jnp.zeros_like(total)
     for load in loads[3:]:
         load.wait()
+    for src, dst in ((target_ref, target_flat), (sign_a_ref, sign_a_flat)):
+        dst[...] = jnp.concatenate(
+            [src[i * sets : (i + 1) * sets, :] for i in range(WIDE)], axis=1
+        )
     for copy in gather_copies:
         copy.wait()
     for d in range(1, n_beta):
@@ -149,62 +158,64 @@
 
     groups = pairs // ROWS
 
-    def excite(p, out, first=0, last=groups):
+    def excite_group(p, out, at):
+        lane = lane_ref[at, :]
+        slot = slot_ref[at, :]
+        sign = sign_ref[at, :]
+        masks = [slot == jnp.int16(d) for d in range(n_beta)]
+        for i in range(WIDE):
+            value = base[p, at, i * cols : (i + 1) * cols]
+            for d in range(1, n_beta):
+                value = jnp.where(masks[d], spread_gather(spread[d, i * sets + p], lane), value)
+            out[at, i * cols : (i + 1) * cols] = value * sign
+
+    def excite(p, out, first, last):
         for g in range(first, last):
-            at = slice(g * ROWS, (g + 1) * ROWS)
-            lane = lane_ref[at, :]
-            slot = slot_ref[at, :]
-            sign = sign_ref[at, :]
-            masks = [slot == jnp.int16(d) for d in range(n_beta)]
-            for i in range(2):
-                value = base[p, at, i * cols : (i + 1) * cols]
-                for d in range(1, n_beta):
-                    value = jnp.where(masks[d], spread_gather(spread[d, 2 * p + i], lane), value)
-                out[at, i * cols : (i + 1) * cols] = value * sign
+            excite_group(p, out, slice(g * ROWS, (g + 1) * ROWS))
+
+    def excite_looped(p, out):
+        def one(g, carry):
+            excite_group(p, out, pl.ds(pl.multiple_of(g * ROWS, ROWS), ROWS))
+            return carry
+
+        lax.fori_loop(0, groups, one, 0)
 
     def contract(src, out):
-        out[...] = jnp.dot(
+        mixed = jnp.dot(
             integrals_ref[...], src[...], preferred_element_type=jnp.float32
         ).astype(jnp.bfloat16)
-
-    iota = lax.broadcasted_iota(jnp.int32, (ROWS, pairs), 0)
-
-    def build(p, out, i):
-        row = pl.ds(2 * p + i, 1)
-        targets = (jnp.broadcast_to(target_ref[row, :], (ROWS, pairs)) - iota).astype(jnp.int16)
+        for i in range(WIDE):
+            out[i * pairs : (i + 1) * pairs, :] = mixed[:, i * cols : (i + 1) * cols]
+
+    iota = lax.broadcasted_iota(jnp.int32, (ROWS, WIDE * pairs), 0)
+
+    def build(p, out):
+        row = pl.ds(p, 1)
+        shape = (ROWS, WIDE * pairs)
+        targets = (jnp.broadcast_to(target_flat[row, :], shape) - iota).astype(jnp.int16)
         signs = (
-            jnp.broadcast_to(sign_a_ref[row, :], (ROWS, pairs))
-            .astype(jnp.float32)
-            .astype(jnp.bfloat16)
+            jnp.broadcast_to(sign_a_flat[row, :], shape).astype(jnp.float32).astype(jnp.bfloat16)
         )
         zero = jnp.zeros_like(signs)
         for k in range(all_alpha // ROWS):
-            out[i, k * ROWS : (k + 1) * ROWS, :] = jnp.where(
+            out[k * ROWS : (k + 1) * ROWS, :] = jnp.where(
                 targets == jnp.int16(k * ROWS), signs, zero
             )
 
-    def scatter(table, src, i):
-        total[...] += jnp.dot(
-            table[i], src[:, i * cols : (i + 1) * cols], preferred_element_type=jnp.float32
-        )
-
-    third = -(-groups // 3)
+    def scatter(table, mixed):
+        total[...] += jnp.dot(table[...], mixed[...], preferred_element_type=jnp.float32)
 
     def stages(p, here, there, mixed, mixed_next, table, table_next):
         contract(there, mixed_next)
-        excite(p + 2, here, 0, third)
-        build(p + 1, table_next, 0)
-        scatter(table, mixed, 0)
-        excite(p + 2, here, third, 2 * third)
-        build(p + 1, table_next, 1)
-        scatter(table, mixed, 1)
-        excite(p + 2, here, 2 * third, groups)
-
-    excite(0, excited_0)
+        excite(p + 2, here, 0, groups // 2)
+        build(p + 1, table_next)
+        scatter(table, mixed)
+        excite(p + 2, here, groups // 2, groups)
+
+    excite_looped(0, excited_0)
     contract(excited_0, mixed_0)
-    build(0, table_0, 0)
-    build(0, table_0, 1)
-    excite(1, excited_1)
+    build(0, table_0)
+    excite_looped(1, excited_1)
 
     def step(s, carry):
         p = 2 * s
@@ -212,13 +223,11 @@
         stages(p + 1, excited_1, excited_0, mixed_1, mixed_0, table_1, table_0)
         return carry
 
-    lax.fori_loop(0, rows // 4 - 1, step, 0)
+    lax.fori_loop(0, sets // 2 - 1, step, 0)
     contract(excited_1, mixed_1)
-    build(rows // 2 - 1, table_1, 0)
-    build(rows // 2 - 1, table_1, 1)
-    for table, mixed in ((table_0, mixed_0), (table_1, mixed_1)):
-        scatter(table, mixed, 0)
-        scatter(table, mixed, 1)
+    build(sets - 1, table_1)
+    scatter(table_0, mixed_0)
+    scatter(table_1, mixed_1)
 
     for i in range(n_alpha):
         outgoing[i] = total[i * rows : (i + 1) * rows, :].astype(jnp.bfloat16)
@@ -263,18 +272,20 @@
             pltpu.VMEM((pairs, cols), jnp.int32),
             pltpu.VMEM((rows, pairs), jnp.int32),
             pltpu.VMEM((rows, pairs), jnp.int32),
+            pltpu.VMEM((rows // WIDE, WIDE * pairs), jnp.int32),
+            pltpu.VMEM((rows // WIDE, WIDE * pairs), jnp.int32),
             pltpu.VMEM((n_beta, rows, cols), jnp.bfloat16),
             pltpu.VMEM((n_beta, rows, ROWS, LANES), jnp.bfloat16),
             pltpu.VMEM((pairs, cols), jnp.int16),
             pltpu.VMEM((pairs, cols), jnp.int16),
             pltpu.VMEM((pairs, cols), jnp.bfloat16),
-            pltpu.VMEM((rows // 2, pairs, 2 * cols), jnp.bfloat16),
-            pltpu.VMEM((pairs, 2 * cols), jnp.bfloat16),
-            pltpu.VMEM((pairs, 2 * cols), jnp.bfloat16),
-            pltpu.VMEM((pairs, 2 * cols), jnp.bfloat16),
-            pltpu.VMEM((pairs, 2 * cols), jnp.bfloat16),
-            pltpu.VMEM((2, all_alpha, pairs), jnp.bfloat16),
-            pltpu.VMEM((2, all_alpha, pairs), jnp.bfloat16),
+            pltpu.VMEM((rows // WIDE, pairs, WIDE * cols), jnp.bfloat16),
+            pltpu.VMEM((pairs, WIDE * cols), jnp.bfloat16),
+            pltpu.VMEM((pairs, WIDE * cols), jnp.bfloat16),
+            pltpu.VMEM((WIDE * pairs, cols), jnp.bfloat16),
+            pltpu.VMEM((WIDE * pairs, cols), jnp.bfloat16),
+            pltpu.VMEM((all_alpha, WIDE * pairs), jnp.bfloat16),
+            pltpu.VMEM((all_alpha, WIDE * pairs), jnp.bfloat16),
             pltpu.VMEM((all_alpha, cols), jnp.float32),
             pltpu.VMEM((n_alpha, rows, cols), jnp.bfloat16),
             pltpu.VMEM((n_alpha - 1, rows, cols), jnp.bfloat16),

time: 19.7 us -> 22.2 us (1.13)
  Pallas kernels: 19 us -> 21.5 us
    pallas_call x1, Pallas kernels: 19 us -> 21.5 us  [on_device(): pl.pallas_call(functools.partial(kernel, n_alpha, n_beta), out_shape=jax....]
where the time goes in v4:
time: 22.2 us; the launch traced here: 22.1 us
  Pallas kernels  21.5 us (97%)
  local copies, waits for them, and re-layouts  0.61 us (3%)
    pallas_call x1, Pallas kernels, on_device(): pl.pallas_call(functools.partial(kernel, n_alpha, n_beta), out_shape=jax....  21.5 us
    unnamed x1, local copies, waits for them, and re-layouts  0.61 us

profile of v4, /device:TPU:0, one launch (start us, length us, event | category | flops | bytes accessed | tf_op | source)
XLA Modules:
  0.0 22.1 jit_solution(15018631659482545468)
XLA Ops:
  0.0 21.5 %shard_map.64 = f32[32,128]{1,0:T(8,128)S(1)} custom-call(bf16[32,128]{1,0:T(8,128)(2,1)} %coeffs_hbm.1, bf16[400,400]{1,0:T(8,128)(2,1)} %integrals_hbm.1, s32[400,128]{1,0:T(8,128)} %source_hbm.1, s32[400,128]{1,0:T(8,128)} %sign_b_hbm.1, s32[32,400]{1,0:T(8,128)} %target_hbm.1, s32[32,400]{1,0:T(8,128)} %sign_a_hbm.1), custom_call_target="tpu_custom_call" | custom-call | tf_op jit(solution)/shard_map/pallas_call | solution.py:264
  21.5 0.6 %copy.8 = f32[32,128]{1,0:T(8,128)} copy(f32[32,128]{1,0:T(8,128)S(1)} %shard_map.64) | data formatting | bytes 32768

commit v5 on v4

--- a/solution.py
+++ b/solution.py
@@ -131,16 +131,20 @@
 
     spread_rows(0)
 
-    def excite_own(g, carry):
-        at = pl.ds(pl.multiple_of(g * ROWS, ROWS), ROWS)
-        lane = lane_ref[at, :]
-        for a in range(rows):
-            base[a % sets, at, (a // sets) * cols : (a // sets + 1) * cols] = spread_gather(
-                spread[0, a], lane
-            )
+    groups = pairs // ROWS
+    together = max(n for n in range(1, 6) if groups % n == 0)
+
+    def excite_own(step, carry):
+        for u in range(together):
+            at = pl.ds(pl.multiple_of((step * together + u) * ROWS, ROWS), ROWS)
+            lane = lane_ref[at, :]
+            for a in range(rows):
+                base[a % sets, at, (a // sets) * cols : (a // sets + 1) * cols] = spread_gather(
+                    spread[0, a], lane
+                )
         return carry
 
-    lax.fori_loop(0, pairs // ROWS, excite_own, 0)
+    lax.fori_loop(0, groups // together, excite_own, 0)
 
     loads[2].wait()
     sign_ref[...] = sign_b_ref[...].astype(jnp.float32).astype(jnp.bfloat16)
@@ -155,8 +159,6 @@
         copy.wait()
     for d in range(1, n_beta):
         spread_rows(d)
-
-    groups = pairs // ROWS
 
     def excite_group(p, out, at):
         lane = lane_ref[at, :]
@@ -173,13 +175,6 @@
         for g in range(first, last):
             excite_group(p, out, slice(g * ROWS, (g + 1) * ROWS))
 
-    def excite_looped(p, out):
-        def one(g, carry):
-            excite_group(p, out, pl.ds(pl.multiple_of(g * ROWS, ROWS), ROWS))
-            return carry
-
-        lax.fori_loop(0, groups, one, 0)
-
     def contract(src, out):
         mixed = jnp.dot(
             integrals_ref[...], src[...], preferred_element_type=jnp.float32
@@ -212,10 +207,10 @@
         scatter(table, mixed)
         excite(p + 2, here, groups // 2, groups)
 
-    excite_looped(0, excited_0)
+    excite(0, excited_0, 0, groups)
     contract(excited_0, mixed_0)
     build(0, table_0)
-    excite_looped(1, excited_1)
+    excite(1, excited_1, 0, groups)
 
     def step(s, carry):
         p = 2 * s

time: 22.2 us -> 18.1 us (0.82)
  Pallas kernels: 21.5 us -> 17.4 us
    pallas_call x1, Pallas kernels: 21.5 us -> 17.4 us  [on_device(): pl.pallas_call(functools.partial(kernel, n_alpha, n_beta), out_shape=jax....]
where the time goes in v5:
time: 18.1 us; the launch traced here: 18 us
  Pallas kernels  17.4 us (96%)
  local copies, waits for them, and re-layouts  0.61 us (3%)
    pallas_call x1, Pallas kernels, on_device(): pl.pallas_call(functools.partial(kernel, n_alpha, n_beta), out_shape=jax....  17.4 us
    unnamed x1, local copies, waits for them, and re-layouts  0.61 us

profile of v5, /device:TPU:0, one launch (start us, length us, event | category | flops | bytes accessed | tf_op | source)
XLA Modules:
  0.0 18.0 jit_solution(2535911932482419503)
XLA Ops:
  0.0 17.4 %shard_map.64 = f32[32,128]{1,0:T(8,128)S(1)} custom-call(bf16[32,128]{1,0:T(8,128)(2,1)} %coeffs_hbm.1, bf16[400,400]{1,0:T(8,128)(2,1)} %integrals_hbm.1, s32[400,128]{1,0:T(8,128)} %source_hbm.1, s32[400,128]{1,0:T(8,128)} %sign_b_hbm.1, s32[32,400]{1,0:T(8,128)} %target_hbm.1, s32[32,400]{1,0:T(8,128)} %sign_a_hbm.1), custom_call_target="tpu_custom_call" | custom-call | tf_op jit(solution)/shard_map/pallas_call | solution.py:259
  17.4 0.6 %copy.8 = f32[32,128]{1,0:T(8,128)} copy(f32[32,128]{1,0:T(8,128)S(1)} %shard_map.64) | data formatting | bytes 32768

commit v6 on v5

--- a/solution.py
+++ b/solution.py
@@ -10,7 +10,7 @@
 MESH = pl.DeviceIdType.MESH
 LANES = 128
 ROWS = 16
-WIDE = 4
+WIDE = 2
 
 
 def spread_gather(values, lanes):
@@ -132,7 +132,7 @@
     spread_rows(0)
 
     groups = pairs // ROWS
-    together = max(n for n in range(1, 6) if groups % n == 0)
+    together = max(n for n in range(1, 26) if groups % n == 0)
 
     def excite_own(step, carry):
         for u in range(together):

time: 18.1 us -> 19.4 us (1.072)
  Pallas kernels: 17.4 us -> 18.6 us
    pallas_call x1, Pallas kernels: 17.4 us -> 18.6 us  [on_device(): pl.pallas_call(functools.partial(kernel, n_alpha, n_beta), out_shape=jax....]
where the time goes in v6:
time: 19.4 us; the launch traced here: 19.2 us
  Pallas kernels  18.6 us (96%)
  local copies, waits for them, and re-layouts  0.61 us (3%)
    pallas_call x1, Pallas kernels, on_device(): pl.pallas_call(functools.partial(kernel, n_alpha, n_beta), out_shape=jax....  18.6 us
    unnamed x1, local copies, waits for them, and re-layouts  0.61 us

profile of v6, /device:TPU:0, one launch (start us, length us, event | category | flops | bytes accessed | tf_op | source)
XLA Modules:
  0.0 19.2 jit_solution(1182438344440274900)
XLA Ops:
  0.0 18.6 %shard_map.64 = f32[32,128]{1,0:T(8,128)S(1)} custom-call(bf16[32,128]{1,0:T(8,128)(2,1)} %coeffs_hbm.1, bf16[400,400]{1,0:T(8,128)(2,1)} %integrals_hbm.1, s32[400,128]{1,0:T(8,128)} %source_hbm.1, s32[400,128]{1,0:T(8,128)} %sign_b_hbm.1, s32[32,400]{1,0:T(8,128)} %target_hbm.1, s32[32,400]{1,0:T(8,128)} %sign_a_hbm.1), custom_call_target="tpu_custom_call" | custom-call | tf_op jit(solution)/shard_map/pallas_call | solution.py:259
  18.6 0.6 %copy.8 = f32[32,128]{1,0:T(8,128)} copy(f32[32,128]{1,0:T(8,128)S(1)} %shard_map.64) | data formatting | bytes 32768

commit v7 on v5

--- a/solution.py
+++ b/solution.py
@@ -10,7 +10,7 @@
 MESH = pl.DeviceIdType.MESH
 LANES = 128
 ROWS = 16
-WIDE = 4
+WIDE = 8
 
 
 def spread_gather(values, lanes):

time: 18.1 us -> 18.3 us (1.011)
  Pallas kernels: 17.4 us -> 17.6 us
    pallas_call x1, Pallas kernels: 17.4 us -> 17.6 us  [on_device(): pl.pallas_call(functools.partial(kernel, n_alpha, n_beta), out_shape=jax....]
where the time goes in v7:
time: 18.3 us; the launch traced here: 18.2 us
  Pallas kernels  17.6 us (96%)
  local copies, waits for them, and re-layouts  0.61 us (3%)
    pallas_call x1, Pallas kernels, on_device(): pl.pallas_call(functools.partial(kernel, n_alpha, n_beta), out_shape=jax....  17.6 us
    unnamed x1, local copies, waits for them, and re-layouts  0.61 us

profile of v7, /device:TPU:0, one launch (start us, length us, event | category | flops | bytes accessed | tf_op | source)
XLA Modules:
  0.0 18.2 jit_solution(5513820572551154361)
XLA Ops:
  0.0 17.6 %shard_map.64 = f32[32,128]{1,0:T(8,128)S(1)} custom-call(bf16[32,128]{1,0:T(8,128)(2,1)} %coeffs_hbm.1, bf16[400,400]{1,0:T(8,128)(2,1)} %integrals_hbm.1, s32[400,128]{1,0:T(8,128)} %source_hbm.1, s32[400,128]{1,0:T(8,128)} %sign_b_hbm.1, s32[32,400]{1,0:T(8,128)} %target_hbm.1, s32[32,400]{1,0:T(8,128)} %sign_a_hbm.1), custom_call_target="tpu_custom_call" | custom-call | tf_op jit(solution)/shard_map/pallas_call | solution.py:259
  17.6 0.6 %copy.8 = f32[32,128]{1,0:T(8,128)} copy(f32[32,128]{1,0:T(8,128)S(1)} %shard_map.64) | data formatting | bytes 32768

commit v8 on v5

--- a/solution.py
+++ b/solution.py
@@ -202,10 +202,9 @@
 
     def stages(p, here, there, mixed, mixed_next, table, table_next):
         contract(there, mixed_next)
-        excite(p + 2, here, 0, groups // 2)
+        scatter(table, mixed)
         build(p + 1, table_next)
-        scatter(table, mixed)
-        excite(p + 2, here, groups // 2, groups)
+        excite(p + 2, here, 0, groups)
 
     excite(0, excited_0, 0, groups)
     contract(excited_0, mixed_0)
@@ -219,8 +218,8 @@
         return carry
 
     lax.fori_loop(0, sets // 2 - 1, step, 0)
+    build(sets - 1, table_1)
     contract(excited_1, mixed_1)
-    build(sets - 1, table_1)
     scatter(table_0, mixed_0)
     scatter(table_1, mixed_1)
 

time: 18.1 us -> 18.1 us (level)
  no operation moved by 1% of the time
where the time goes in v8:
time: 18.1 us; the launch traced here: 18 us
  Pallas kernels  17.4 us (96%)
  local copies, waits for them, and re-layouts  0.61 us (3%)
    pallas_call x1, Pallas kernels, on_device(): pl.pallas_call(functools.partial(kernel, n_alpha, n_beta), out_shape=jax....  17.4 us
    unnamed x1, local copies, waits for them, and re-layouts  0.61 us

profile of v8, /device:TPU:0, one launch (start us, length us, event | category | flops | bytes accessed | tf_op | source)
XLA Modules:
  0.0 18.0 jit_solution(2535911932482419503)
XLA Ops:
  0.0 17.4 %shard_map.64 = f32[32,128]{1,0:T(8,128)S(1)} custom-call(bf16[32,128]{1,0:T(8,128)(2,1)} %coeffs_hbm.1, bf16[400,400]{1,0:T(8,128)(2,1)} %integrals_hbm.1, s32[400,128]{1,0:T(8,128)} %source_hbm.1, s32[400,128]{1,0:T(8,128)} %sign_b_hbm.1, s32[32,400]{1,0:T(8,128)} %target_hbm.1, s32[32,400]{1,0:T(8,128)} %sign_a_hbm.1), custom_call_target="tpu_custom_call" | custom-call | tf_op jit(solution)/shard_map/pallas_call | solution.py:258
  17.4 0.6 %copy.8 = f32[32,128]{1,0:T(8,128)} copy(f32[32,128]{1,0:T(8,128)S(1)} %shard_map.64) | data formatting | bytes 32768
